TPU v7x, 512 devices: a whole 4x8x8 slice. The times are simulated.
512 devices in a mesh: chain: 8 (over y), sector: 16 (over z, core), term: 4 (over x).
Axes of the slice: x: 4, y: 8, z: 8, core: 2. Of those that a mesh axis runs over, the one named last changes fastest.
Arguments:
- two_site: float32 [8, 16, 256, 256], P('chain', 'sector'), may hold values from -6 to 6
- left_env: bfloat16 [8, 40, 16, 256, 256], P('chain', 'term', 'sector'), may hold values from -1 to 2
- right_env: bfloat16 [8, 40, 16, 256, 256], P('chain', 'term', 'sector'), may hold values from -1 to 2
- block_dims: int32 [16], P('sector'), may hold values from 128 to 256, as said below
- sources: int32 [40, 16, 3], P('term', 'sector'), may hold values from 0 to 15, as said below
- sixj_index: int32 [40, 16, 3], P('term', 'sector'), may hold values from 0 to 63, as said below
- sixj_table: float32 [64], replicated, may hold values from -1 to 1
Outputs:
- solution: bfloat16 [8, 16, 256, 256], P('chain', 'sector')
- energy: float32 [8], P('chain')
- handoff: bfloat16 [8, 40, 16, 256, 256], P('chain', 'term', 'sector')
Inputs may be any that keep to these rules, and one draw needn't show every extreme that they name: `block_dims`: at least one sector block has dimension 256. sources[w, b, 0] = b for every term w and sector b. sixj_index[w, b, 0] < 16 for every term w and sector b.
All inputs are finite; a program needn't handle non-finite values.
Results may differ from a plain program's by a relative error of at most 0.03.
Values may be sent and summed in bfloat16 or wider, within the bound.
A program may use at most 64 MiB of HBM per device.

v0:
```python
import math

import jax
import jax.numpy as jnp
from jax import lax
from jax.sharding import PartitionSpec as P

ITERS = 4


step_size = 0.1
epsilon = 1e-06


def shifted(value, axis, steps):
    count = lax.axis_size(axis)
    leading, last = (max(0, -steps), min(count, count - steps))
    return lax.ppermute(value, axis, [(source, source + steps) for source in range(leading, last)])


def coefficients(sources, sixj_index, sixj_table, sector_count):
    levels = jnp.arange(sixj_table.shape[0], dtype=jnp.int32)
    picked = jnp.sum(
        jnp.where(sixj_index[..., None] == levels, sixj_table, jnp.zeros_like(sixj_table)), axis=-1
    )
    sectors = jnp.arange(sector_count, dtype=jnp.int32)
    spread = jnp.where(
        sources[..., None] == sectors, picked[..., None], jnp.zeros_like(picked[..., None])
    )
    return jnp.sum(spread, axis=2).astype(jnp.bfloat16)


def local(two_site, left_env, right_env, block_dims, sources, sixj_index, sixj_table):
    start_state = two_site[0]
    left_blocks = left_env[0]
    right_blocks = right_env[0]
    blocks = start_state.shape[0]
    width = start_state.shape[1]
    sector_count = blocks * lax.axis_size("sector")
    volume = float(sector_count * width * width)
    coupling = coefficients(sources, sixj_index, sixj_table, sector_count)
    row_mask = (jnp.arange(width, dtype=jnp.int32)[None, :] < block_dims[:, None]).astype(
        jnp.float32
    )
    mask = row_mask[:, :, None] * row_mask[:, None, :]

    def reduce_image(partial_value):
        return lax.psum(partial_value.astype(jnp.bfloat16), "term").astype(jnp.float32)

    def totals(stacked):
        return lax.psum(stacked, "sector")

    def partial_image(rounded_whole):
        gathered = lax.all_gather(rounded_whole, "sector", axis=0, tiled=True)
        mixed = jnp.einsum(
            "wba,aij->wbij", coupling, gathered, preferred_element_type=jnp.float32
        ).astype(jnp.bfloat16)
        right_part = jnp.einsum(
            "wbij,wbjk->wbik", mixed, right_blocks, preferred_element_type=jnp.float32
        ).astype(jnp.bfloat16)
        return jnp.einsum(
            "wbij,wbjk->bik", left_blocks, right_part, preferred_element_type=jnp.float32
        )

    def image_of(state):
        rounded_whole = state.astype(jnp.bfloat16)
        image = reduce_image(partial_image(rounded_whole)) * mask
        return (rounded_whole, image)

    state = start_state * mask
    squares = totals(jnp.stack([jnp.sum(state * state)]))[0]
    state = state * lax.rsqrt(squares / volume + epsilon)
    for iteration in range(ITERS):
        rounded_whole, image = image_of(state)
        summed = totals(jnp.stack([jnp.sum(state * image), jnp.sum(state * state)]))
        rayleigh = summed[0] / summed[1]
        state = state - step_size * (image - rayleigh * state)
        squares = totals(jnp.stack([jnp.sum(state * state)]))[0]
        state = state * lax.rsqrt(squares / volume + epsilon)
    rounded_whole, image = image_of(state)
    summed = totals(jnp.stack([jnp.sum(state * image), jnp.sum(state * state)]))
    energy = summed[0] / summed[1]
    inner = jnp.einsum(
        "wbij,bjk->wbik", left_blocks, rounded_whole, preferred_element_type=jnp.float32
    ).astype(jnp.bfloat16)
    fresh = jnp.einsum(
        "bji,wbjk->wbik", rounded_whole, inner, preferred_element_type=jnp.float32
    ) / math.sqrt(width)
    received = shifted(fresh.astype(jnp.bfloat16), "chain", 1)
    handoff = jnp.where(lax.axis_index("chain") == 0, left_blocks, received)
    return (rounded_whole[None], energy.reshape(1), handoff[None])


def solution(mesh):
    return jax.shard_map(
        local,
        mesh=mesh,
        in_specs=(
            P("chain", "sector", None, None),
            P("chain", "term", "sector", None, None),
            P("chain", "term", "sector", None, None),
            P("sector"),
            P("term", "sector", None),
            P("term", "sector", None),
            P(),
        ),
        out_specs=(
            P("chain", "sector", None, None),
            P("chain"),
            P("chain", "term", "sector", None, None),
        ),
        check_vma=False,
    )
```

profile of v0, /device:TPU:24, one launch (start us, length us, event | category | flops | bytes accessed | tf_op | source)
XLA Modules:
  0.0 811.9 jit_solution(5907305467150563734)
XLA Ops:
  8.0 1.1 copy.29
  9.1 0.7 multiply_reduce_fusion.13
  9.8 32.6 %psum.105 = f32[1]{0:T(128)} all-reduce(f32[1]{0:T(128)} %bitcast.2), channel_id=1, replica_groups=mesh['chain'=8,'sector'=16,'term'=4] {'sector'}, use_global_device_ids=true, to_apply=%region_1.2 | all-reduce | flops 1 | bytes 8 | tf_op jit(solution)/shard_map/psum | solution.py:51
  43.3 0.8 copy.32
  44.3 0.2 fusion.170
  44.7 38.6 %all-gather.6.cloned.1.call-done = bf16[16,256,256]{2,1,0:T(8,128)(2,1)} async-done(((bf16[1,256,256]{2,1,0:T(8,128)(2,1)}), bf16[16,256,256]{2,1,0:T(8,128)(2,1)}) %all-gather.6.cloned.1.call-update) | async-done | bytes 2097168 | tf_op jit(solution)/shard_map/all_gather | solution.py:54
  83.3 4.2 fusion.10
  87.5 3.6 fusion.158
  91.1 50.0 %all-reduce.6.cloned.1.call-done = bf16[1,256,256]{1,2,0:T(8,128)(2,1)} async-done(((bf16[1,256,256]{1,2,0:T(8,128)(2,1)}), bf16[1,256,256]{1,2,0:T(8,128)(2,1)}) %all-reduce.6.cloned.1.call-update) | async-done | bytes 131088 | tf_op jit(solution)/shard_map/psum | solution.py:48
  141.2 1.7 multiply_reduce_fusion.12
  142.9 1.4 pad_maximum_fusion
  144.2 24.8 %psum.107 = f32[2]{0:T(128)S(1)} all-reduce(f32[2]{0:T(128)S(1)} %pad_maximum_fusion), channel_id=1, replica_groups=mesh['chain'=8,'sector'=16,'term'=4] {'sector'}, use_global_device_ids=true, to_apply=%region_7.8 | all-reduce | flops 2 | bytes 16 | tf_op jit(solution)/shard_map/psum | solution.py:51
  169.1 0.6 fusion.182
  171.0 1.7 multiply_reduce_fusion.10
  172.7 24.2 %psum.108 = f32[1]{0:T(128)} all-reduce(f32[1]{0:T(128)} %bitcast.15), channel_id=1, replica_groups=mesh['chain'=8,'sector'=16,'term'=4] {'sector'}, use_global_device_ids=true, to_apply=%region_9.10 | all-reduce | flops 1 | bytes 8 | tf_op jit(solution)/shard_map/psum | solution.py:51
  197.6 0.8 copy.36
  198.4 42.5 %all-gather.8.cloned.1.call-done = bf16[16,256,256]{2,1,0:T(8,128)(2,1)} async-done(((bf16[1,256,256]{2,1,0:T(8,128)(2,1)}), bf16[16,256,256]{2,1,0:T(8,128)(2,1)}) %all-gather.8.cloned.1.call-update) | async-done | bytes 2097168 | tf_op jit(solution)/shard_map/all_gather | solution.py:54
  240.9 4.2 fusion.13
  245.1 3.6 fusion.151
  248.7 50.0 %all-reduce.8.cloned.1.call-done = bf16[1,256,256]{1,2,0:T(8,128)(2,1)} async-done(((bf16[1,256,256]{1,2,0:T(8,128)(2,1)}), bf16[1,256,256]{1,2,0:T(8,128)(2,1)}) %all-reduce.8.cloned.1.call-update) | async-done | bytes 131088 | tf_op jit(solution)/shard_map/psum | solution.py:48
  298.8 1.7 multiply_reduce_fusion.9
  300.4 1.4 pad_maximum_fusion.1
  301.8 24.8 %psum.110 = f32[2]{0:T(128)S(1)} all-reduce(f32[2]{0:T(128)S(1)} %pad_maximum_fusion.1), channel_id=1, replica_groups=mesh['chain'=8,'sector'=16,'term'=4] {'sector'}, use_global_device_ids=true, to_apply=%region_13.14 | all-reduce | flops 2 | bytes 16 | tf_op jit(solution)/shard_map/psum | solution.py:51
  326.6 0.6 fusion.181
  328.6 1.7 multiply_reduce_fusion.7
  330.2 24.2 %psum.111 = f32[1]{0:T(128)} all-reduce(f32[1]{0:T(128)} %bitcast.23), channel_id=1, replica_groups=mesh['chain'=8,'sector'=16,'term'=4] {'sector'}, use_global_device_ids=true, to_apply=%region_15.16 | all-reduce | flops 1 | bytes 8 | tf_op jit(solution)/shard_map/psum | solution.py:51
  355.1 0.8 copy.40
  356.0 42.5 %all-gather.10.cloned.1.call-done = bf16[16,256,256]{2,1,0:T(8,128)(2,1)} async-done(((bf16[1,256,256]{2,1,0:T(8,128)(2,1)}), bf16[16,256,256]{2,1,0:T(8,128)(2,1)}) %all-gather.10.cloned.1.call-update) | async-done | bytes 2097168 | tf_op jit(solution)/shard_map/all_gather | solution.py:54
  398.4 4.2 fusion.16
  402.7 3.6 fusion.144
  406.3 50.0 %all-reduce.10.cloned.1.call-done = bf16[1,256,256]{1,2,0:T(8,128)(2,1)} async-done(((bf16[1,256,256]{1,2,0:T(8,128)(2,1)}), bf16[1,256,256]{1,2,0:T(8,128)(2,1)}) %all-reduce.10.cloned.1.call-update) | async-done | bytes 131088 | tf_op jit(solution)/shard_map/psum | solution.py:48
  456.3 1.7 multiply_reduce_fusion.6
  458.0 1.4 pad_maximum_fusion.2
  459.3 24.8 %psum.113 = f32[2]{0:T(128)S(1)} all-reduce(f32[2]{0:T(128)S(1)} %pad_maximum_fusion.2), channel_id=1, replica_groups=mesh['chain'=8,'sector'=16,'term'=4] {'sector'}, use_global_device_ids=true, to_apply=%region_19.20 | all-reduce | flops 2 | bytes 16 | tf_op jit(solution)/shard_map/psum | solution.py:51
  484.2 0.6 fusion.180
  486.1 1.7 multiply_reduce_fusion.4
  487.8 24.2 %psum.114 = f32[1]{0:T(128)} all-reduce(f32[1]{0:T(128)} %bitcast.31), channel_id=1, replica_groups=mesh['chain'=8,'sector'=16,'term'=4] {'sector'}, use_global_device_ids=true, to_apply=%region_21.22 | all-reduce | flops 1 | bytes 8 | tf_op jit(solution)/shard_map/psum | solution.py:51
  512.7 0.8 copy.44
  513.5 0.2 all-reduce.12.cloned.1.call-start
  513.7 42.3 %all-gather.12.cloned.1.call-done = bf16[16,256,256]{2,1,0:T(8,128)(2,1)} async-done(((bf16[1,256,256]{2,1,0:T(8,128)(2,1)}), bf16[16,256,256]{2,1,0:T(8,128)(2,1)}) %all-gather.12.cloned.1.call-update) | async-done | bytes 2097168 | tf_op jit(solution)/shard_map/all_gather | solution.py:54
  556.0 4.2 fusion.19
  560.2 3.6 fusion.137
  563.8 50.0 %all-reduce.12.cloned.1.call-done = bf16[1,256,256]{1,2,0:T(8,128)(2,1)} async-done(((bf16[1,256,256]{1,2,0:T(8,128)(2,1)}), bf16[1,256,256]{1,2,0:T(8,128)(2,1)}) %all-reduce.12.cloned.1.call-update) | async-done | bytes 131088 | tf_op jit(solution)/shard_map/psum | solution.py:48
  613.9 1.7 multiply_reduce_fusion.3
  615.5 1.4 pad_maximum_fusion.3
  616.9 24.8 %psum.116 = f32[2]{0:T(128)S(1)} all-reduce(f32[2]{0:T(128)S(1)} %pad_maximum_fusion.3), channel_id=1, replica_groups=mesh['chain'=8,'sector'=16,'term'=4] {'sector'}, use_global_device_ids=true, to_apply=%region_25.26 | all-reduce | flops 2 | bytes 16 | tf_op jit(solution)/shard_map/psum | solution.py:51
  641.7 0.6 fusion.179
  643.7 1.7 multiply_reduce_fusion.1
  645.4 24.2 %psum.117 = f32[1]{0:T(128)} all-reduce(f32[1]{0:T(128)} %bitcast.39), channel_id=1, replica_groups=mesh['chain'=8,'sector'=16,'term'=4] {'sector'}, use_global_device_ids=true, to_apply=%region_27.28 | all-reduce | flops 1 | bytes 8 | tf_op jit(solution)/shard_map/psum | solution.py:51
  670.2 0.8 copy.48
  671.1 1.9 fusion.31
  673.0 4.6 collective-permute-start
  677.6 1.6 copy.52
  679.2 0.8 copy.54
  680.0 33.4 %all-gather.14.cloned.1.call-done = bf16[16,256,256]{2,1,0:T(8,128)(2,1)} async-done(((bf16[1,256,256]{2,1,0:T(8,128)(2,1)}), bf16[16,256,256]{2,1,0:T(8,128)(2,1)}) %all-gather.14.cloned.1.call-update) | async-done | bytes 2097168 | tf_op jit(solution)/shard_map/all_gather | solution.py:54
  713.4 4.2 fusion.22
  717.6 3.9 fusion.130
  721.6 2.5 fusion.32
  724.1 47.5 %all-reduce.14.cloned.1.call-done = bf16[1,256,256]{1,2,0:T(8,128)(2,1)} async-done(((bf16[1,256,256]{1,2,0:T(8,128)(2,1)}), bf16[1,256,256]{1,2,0:T(8,128)(2,1)}) %all-reduce.14.cloned.1.call-update) | async-done | bytes 131088 | tf_op jit(solution)/shard_map/psum | solution.py:48
  771.6 1.7 fusion.166
  773.3 1.4 pad_maximum_fusion.4
  774.7 2.4 copy.55
  777.1 24.8 %psum.119 = f32[2]{0:T(128)S(1)} all-reduce(f32[2]{0:T(128)S(1)} %pad_maximum_fusion.4), channel_id=1, replica_groups=mesh['chain'=8,'sector'=16,'term'=4] {'sector'}, use_global_device_ids=true, to_apply=%region_31.32 | all-reduce | flops 2 | bytes 16 | tf_op jit(solution)/shard_map/psum | solution.py:51
  801.9 0.6 fusion.178
  (40 shorter events, 1.1 us)
Async XLA Ops:
  7.2 80.3 %copy-start = (bf16[1,10,1,256,256]{4,3,2,1,0:T(8,128)(2,1)S(1)}, bf16[1,10,1,256,256]{4,3,2,1,0:T(8,128)(2,1)}, u32[]{:S(2)}) copy-start(bf16[1,10,1,256,256]{4,3,2,1,0:T(8,128)(2,1)} %param.9) | copy-start | bytes 3932164
  7.2 36.9 %copy-start.2 = (s32[10,1,3]{0,1,2:T(1,128)S(1)}, s32[10,1,3]{0,1,2:T(1,128)}, u32[]{:S(2)}) copy-start(s32[10,1,3]{0,1,2:T(1,128)} %param.11) | copy-start | bytes 364
  7.2 37.0 %copy-start.3 = (s32[10,1,3]{0,1,2:T(1,128)S(1)}, s32[10,1,3]{0,1,2:T(1,128)}, u32[]{:S(2)}) copy-start(s32[10,1,3]{0,1,2:T(1,128)} %param.12) | copy-start | bytes 364
  7.2 37.1 %copy-start.4 = (f32[64]{0:T(128)S(1)}, f32[64]{0:T(128)}, u32[]{:S(2)}) copy-start(f32[64]{0:T(128)} %param.13) | copy-start | bytes 772
  7.2 76.1 %all-gather.6.cloned.1.call-start = ((), (), s32[]{:S(2)}) async-start(), calls=%async_computation | async-start | bytes 2228224 | tf_op jit(solution)/shard_map/all_gather | solution.py:54
  44.0 97.1 %all-reduce.6.cloned.1.call-start = ((), (), s32[]{:S(2)}) async-start(), calls=%async_computation.1 | async-start | bytes 262144 | tf_op jit(solution)/shard_map/psum | solution.py:48
  44.7 42.9 %copy-start.1 = (bf16[1,10,1,256,256]{4,3,2,1,0:T(8,128)(2,1)S(1)}, bf16[1,10,1,256,256]{4,3,2,1,0:T(8,128)(2,1)}, u32[]{:S(2)}) copy-start(bf16[1,10,1,256,256]{4,3,2,1,0:T(8,128)(2,1)} %param.8) | copy-start | bytes 3932164
  91.1 149.8 %all-gather.8.cloned.1.call-start = ((), (), s32[]{:S(2)}) async-start(), calls=%async_computation.2 | async-start | bytes 2228224 | tf_op jit(solution)/shard_map/all_gather | solution.py:54
  198.4 100.4 %all-reduce.8.cloned.1.call-start = ((), (), s32[]{:S(2)}) async-start(), calls=%async_computation.3 | async-start | bytes 262144 | tf_op jit(solution)/shard_map/psum | solution.py:48
  248.7 149.8 %all-gather.10.cloned.1.call-start = ((), (), s32[]{:S(2)}) async-start(), calls=%async_computation.4 | async-start | bytes 2228224 | tf_op jit(solution)/shard_map/all_gather | solution.py:54
  355.9 100.4 %all-reduce.10.cloned.1.call-start = ((), (), s32[]{:S(2)}) async-start(), calls=%async_computation.5 | async-start | bytes 262144 | tf_op jit(solution)/shard_map/psum | solution.py:48
  406.2 149.8 %all-gather.12.cloned.1.call-start = ((), (), s32[]{:S(2)}) async-start(), calls=%async_computation.6 | async-start | bytes 2228224 | tf_op jit(solution)/shard_map/all_gather | solution.py:54
  513.5 100.4 %all-reduce.12.cloned.1.call-start = ((), (), s32[]{:S(2)}) async-start(), calls=%async_computation.7 | async-start | bytes 262144 | tf_op jit(solution)/shard_map/psum | solution.py:48
  563.8 149.6 %all-gather.14.cloned.1.call-start = ((), (), s32[]{:S(2)}) async-start(), calls=%async_computation.8 | async-start | bytes 2228224 | tf_op jit(solution)/shard_map/all_gather | solution.py:54
  671.0 100.6 %all-reduce.14.cloned.1.call-start = ((), (), s32[]{:S(2)}) async-start(), calls=%async_computation.9 | async-start | bytes 262144 | tf_op jit(solution)/shard_map/psum | solution.py:48
  673.0 48.5 %collective-permute-start = (bf16[10,1,256,256]{2,3,0,1:T(8,128)(2,1)}, bf16[10,1,256,256]{2,3,0,1:T(8,128)(2,1)}, u32[]{:S(2)}, u32[]{:S(2)}) collective-permute-start(bf16[10,1,256,256]{2,3,0,1:T(8,128)(2,1)} %fusion.31), channel_id=1, source_target_pairs={{0,64},{64,128},{128,192},{192,256},{256,320},{320,384},{384,448},... | collective-permute-start | bytes 3932168 | tf_op jit(solution)/shard_map/ppermute | solution.py:18
Sparse Core Ops, SparseCore 0:
  44.2 39.0 all-gather.5
  91.2 49.9 all-reduce.5
  198.5 42.3 all-gather.7
  248.8 49.9 all-reduce.7
  356.0 42.3 all-gather.9
  406.4 49.9 all-reduce.9
  513.6 42.3 all-gather.11
  563.9 49.9 all-reduce.11
  671.1 42.2 all-gather.13
  721.7 49.9 all-reduce.13
where the time goes:
time: 814 us; the launch traced here: 812 us
  waiting for transfers between devices  447 us (55%)
  blocking collectives  253 us (31%)
  matrix products  41.2 us (5%)
  between operations  26.4 us (3%)
  other arithmetic  25.7 us (3%)
  local copies, waits for them, and re-layouts  12.8 us (2%)
    psum x10, blocking collectives, totals(): return lax.psum(stacked, 'sector')  253 us
    psum x5, waiting for transfers between devices, reduce_image(): lax.psum(partial_value.astype(jnp.bfloat16), 'term').astype(jnp.float32)  248 us
    all_gather x5, waiting for transfers between devices, partial_image(): gathered = lax.all_gather(rounded_whole, 'sector', axis=0, tiled=True)  199 us
    dot_general x5, matrix products, partial_image(): jnp.einsum('wba,aij->wbij', coupling, gathered, preferred_element_type=jn...  21 us
    dot_general x5, matrix products, partial_image(): jnp.einsum('wbij,wbjk->bik', left_blocks, right_part, preferred_element_t...  18.2 us
  transfers between devices with their start and end apart: 11, of which 10 were waited for; matrix products, arithmetic and copies ran while one was open for 2% of the time, Pallas kernels for 0%

commit v1 on v0

v1 whole, which is shorter than its diff:
```python
import jax
import jax.numpy as jnp
from jax import lax
from jax.experimental import pallas as pl
from jax.experimental.pallas import tpu as pltpu
from jax.sharding import PartitionSpec as P

ITERS = 4
STEP = 0.1
EPSILON = 1e-06
MESH = pl.DeviceIdType.MESH
F32 = jnp.float32
BF16 = jnp.bfloat16


def place(distance, ring):
    half = ring // 2
    return jnp.where(
        distance == 0,
        0,
        jnp.where(
            distance < half,
            2 * distance - 1,
            jnp.where(distance == half, ring - 1, 2 * (ring - distance)),
        ),
    )


def place_static(distance, ring):
    half = ring // 2
    if distance == 0:
        return 0
    if distance < half:
        return 2 * distance - 1
    return ring - 1 if distance == half else 2 * (ring - distance)


def build(segments, sectors, terms_axis, terms, couplings, width):
    ring = sectors // 2
    quarter = width // terms_axis
    gathers = ITERS + 1
    volume = float(sectors * width * width)
    chunks = [(0, 1)]
    for reach in range(1, ring // 2):
        chunks.append((2 * reach - 1, 2))
    start, size = chunks.pop()
    chunks.append((start, size + 1))
    n_chunks = len(chunks)

    def kernel(
        two_site, left_hbm, right_hbm, dims, sources, sixj_index, sixj_table,
        solution_out, energy_out, handoff_out,
        left, right, previous, g0, g1, g2, g3, g4, mixed, part, outgoing, arrived,
        state_ref, image_ref, next_ref, scalars, scalars_term, block, previous_block,
        load_sem, left_sems, z_sems, x_sems, core_sems, rs_sems, sz_sems, sx_sems, sol_sems, sol_y_sems,
    ):
        gathered = (g0, g1, g2, g3, g4)
        y = lax.axis_index("chain")
        b = lax.axis_index("sector")
        t = lax.axis_index("term")
        z = b // 2
        c = b % 2

        def wrap(value, count):
            return lax.rem(value + count, count)

        def at_term(step):
            return (y, b, wrap(t + step, terms_axis))

        def at_sector(dz, dc):
            return (y, wrap(z + dz, ring) * 2 + wrap(c + dc, 2), t)

        def at_segment(dy, dt):
            return (wrap(y + dy, segments), b, wrap(t + dt, terms_axis))

        term_steps = (1, terms_axis - 1) + tuple(range(2, terms_axis - 1))
        sector_steps = [(dz, dc) for dz in range(ring) for dc in range(2) if (dz, dc) != (0, 0)]
        my_rows = pl.ds(pl.multiple_of(t * quarter, quarter), quarter)

        def rows_of(step):
            owner = wrap(t + step, terms_axis)
            return pl.ds(pl.multiple_of(owner * quarter, quarter), quarter)

        load_left = pltpu.make_async_copy(left_hbm.at[0, :, 0], left, load_sem.at[0])
        load_right = pltpu.make_async_copy(right_hbm.at[0, :, 0], right, load_sem.at[1])
        load_right.start()
        load_left.start()

        barrier = pltpu.get_barrier_semaphore()
        for step in term_steps:
            pl.semaphore_signal(barrier, inc=1, device_id=at_term(step), device_id_type=MESH)
        for dz, dc in sector_steps:
            pl.semaphore_signal(barrier, inc=1, device_id=at_sector(dz, dc), device_id_type=MESH)
        for dt in range(terms_axis):
            pl.semaphore_signal(barrier, inc=1, device_id=at_segment(-1, dt), device_id_type=MESH)

        def remote(source, target, sems, index, device):
            copy = pltpu.make_async_remote_copy(
                src_ref=source,
                dst_ref=target,
                send_sem=sems.at[(0,) + index],
                recv_sem=sems.at[(1,) + index],
                device_id=device,
                device_id_type=MESH,
            )
            copy.start()
            return copy

        limit = dims[0]
        row_ids = lax.broadcasted_iota(jnp.int32, (quarter, width), 0) + t * quarter
        column_ids = lax.broadcasted_iota(jnp.int32, (quarter, width), 1)
        mask = jnp.where((row_ids < limit) & (column_ids < limit), 1.0, 0.0).astype(F32)

        state = two_site[0, 0, my_rows, :] * mask
        state_ref[...] = state
        gathered[0][0, my_rows, :] = state.astype(BF16)

        pl.semaphore_wait(barrier, len(term_steps) + len(sector_steps) + terms_axis)

        def send_scalars(k, rows):
            blank = jnp.zeros((8 - len(rows), 128), F32)
            scalars[k, b] = jnp.concatenate(rows + [blank], axis=0)
            return [
                remote(scalars.at[k, b], scalars.at[k, b], sz_sems, (k % 2, i), at_sector(dz, dc))
                for i, (dz, dc) in enumerate(sector_steps)
            ]

        def pass_scalars(k, copies):
            for copy in copies:
                copy.wait()
            scalars_term[k, t] = jnp.sum(scalars[k], axis=0)
            return [
                remote(scalars_term.at[k, t], scalars_term.at[k, t], sx_sems, (k % 2, i), at_term(step))
                for i, step in enumerate(term_steps)
            ]

        def take_scalars(k, copies):
            for copy in copies:
                copy.wait()
            return jnp.sum(jnp.sum(scalars_term[k], axis=0), axis=1, keepdims=True)

        def fold(value):
            columns = jnp.sum(value, axis=0, keepdims=True)
            total = columns[:, 0:128]
            for first in range(128, width, 128):
                total = total + columns[:, first : first + 128]
            return total

        def gather(k, scalar_rows):
            whole = gathered[k]
            parity = k % 2
            z_copies = {}
            for distance in sorted(range(1, ring), key=lambda d: place_static(d, ring)):
                z_copies[distance] = remote(
                    whole.at[0, my_rows],
                    whole.at[place_static(ring - distance, ring), my_rows],
                    z_sems, (parity, distance - 1), at_sector(distance, 0),
                )
            x_copies, core_copies = {}, []

            def spread(index):
                first, count = chunks[index]
                for i, step in enumerate(term_steps):
                    piece = whole.at[pl.ds(first, count), my_rows]
                    x_copies[index, i] = remote(piece, piece, x_sems, (parity, i, index), at_term(step))
                core_copies.append(
                    remote(
                        whole.at[pl.ds(first, count), my_rows],
                        whole.at[pl.ds(ring + first, count), my_rows],
                        core_sems, (parity, 0, index), at_sector(0, 1),
                    )
                )

            spread(0)
            scalar_copies = send_scalars(k - 1, scalar_rows) if k else None
            for index in range(1, n_chunks):
                first, count = chunks[index]
                for distance in range(1, ring):
                    if first <= place_static(ring - distance, ring) < first + count:
                        z_copies[distance].wait_recv()
                spread(index)
            if k:
                scalar_copies = pass_scalars(k - 1, scalar_copies)
            for index in range(n_chunks):
                first, count = chunks[index]
                for i, step in enumerate(term_steps):
                    x_copies[index, i].wait_recv()
                    rows = rows_of(-step)
                    core_copies.append(
                        remote(
                            whole.at[pl.ds(first, count), rows],
                            whole.at[pl.ds(ring + first, count), rows],
                            core_sems, (parity, 1 + i, index), at_sector(0, 1),
                        )
                    )
            totals = take_scalars(k - 1, scalar_copies) if k else None
            for copy in core_copies:
                copy.wait_recv()
            sent = list(z_copies.values()) + list(x_copies.values()) + core_copies
            return totals, sent

        def sector_place(sector):
            return wrap(sector % 2 + c, 2) * ring + place(wrap(sector // 2 - z + ring, ring), ring)

        def apply_terms(whole):
            part[...] = jnp.zeros_like(part)

            def one(w, _):
                spots = [sector_place(sources[w, 0, i]) for i in range(couplings)]
                weights = [sixj_table[sixj_index[w, 0, i]] for i in range(couplings)]
                for first in range(0, width, 64):
                    rows = pl.ds(first, 64)
                    total = weights[0] * whole[spots[0], rows, :].astype(F32)
                    for i in range(1, couplings):
                        total = total + weights[i] * whole[spots[i], rows, :].astype(F32)
                    mixed[rows, :] = total.astype(BF16)
                right_part = jnp.dot(mixed[...], right[w], preferred_element_type=F32).astype(BF16)
                part[...] += jnp.dot(left[w], right_part, preferred_element_type=F32)
                return 0

            lax.fori_loop(0, terms, one, 0)

        def reduce_image(k):
            outgoing[...] = part[...].astype(BF16)
            copies = [
                remote(outgoing.at[rows_of(step)], arrived.at[k, i], rs_sems, (k % 2, i), at_term(step))
                for i, step in enumerate(term_steps)
            ]
            total = part[my_rows, :]
            for i, copy in enumerate(copies):
                copy.wait()
                total = total + arrived[k, i].astype(F32)
            return total * mask

        def corrected(k, totals, scale, shift):
            norm, cross, square = totals[0:1], totals[1:2], totals[2:3]
            delta = 1.0 - cross / norm
            grown = square + 2.0 * delta * cross + delta * delta * norm
            if k == 0:
                scale = lax.rsqrt(norm / volume + EPSILON)
                sigma = scale * lax.rsqrt(scale * scale * (grown / volume) + EPSILON)
            else:
                sigma = lax.rsqrt(grown / volume + EPSILON)
            return delta, sigma, shift + delta

        load_left.wait()
        left_copy = remote(left, previous, left_sems, (), at_segment(1, 0))
        load_right.wait()

        shift = jnp.zeros((1, 1), F32)
        rows = None
        for k in range(ITERS):
            totals, sent = gather(k, rows)
            if k:
                delta, sigma, shift = corrected(k - 1, totals, None, shift)
                state_ref[...] = sigma * (next_ref[...] + delta * state_ref[...])
            apply_terms(gathered[k])
            image = reduce_image(k)
            if k:
                image = sigma * (image + delta * image_ref[...])
            image_ref[...] = image
            state = state_ref[...]
            following = (1.0 + shift) * state - STEP * image
            next_ref[...] = following
            gathered[k + 1][0, my_rows, :] = following.astype(BF16)
            rows = [fold(state * state), fold(following * state), fold(following * following)]
            for copy in sent:
                copy.wait_send()

        totals, sent = gather(ITERS, rows)
        delta, sigma, shift = corrected(ITERS - 1, totals, None, shift)
        state = sigma * (next_ref[...] + delta * state_ref[...])
        block[my_rows, :] = state.astype(BF16)
        block_copies = [
            remote(block.at[my_rows], block.at[my_rows], sol_sems, (i,), at_term(step))
            for i, step in enumerate(term_steps)
        ]
        onward = [
            remote(block.at[my_rows], previous_block.at[my_rows], sol_y_sems, (dt,), at_segment(1, dt))
            for dt in range(terms_axis)
        ]
        apply_terms(gathered[ITERS])
        for copy in block_copies:
            copy.wait()
        solution_out[0, 0] = block[...]
        overlap = fold(part[...] * block[...].astype(F32)) + fold(delta * state * image_ref[...])
        energy_copies = send_scalars(ITERS, [fold(state * state), sigma * overlap])
        for copy in sent:
            copy.wait_send()

        left_copy.wait()
        for copy in onward:
            copy.wait()
        energy_copies = pass_scalars(ITERS, energy_copies)

        @pl.when(y == 0)
        def _():
            handoff_out[0, :, 0] = left[...]

        @pl.when(y != 0)
        def _():
            mixed[...] = previous_block[...].T

            def one(w, _):
                inner = jnp.dot(previous[w], previous_block[...], preferred_element_type=F32).astype(BF16)
                fresh = jnp.dot(mixed[...], inner, preferred_element_type=F32) * (1.0 / width**0.5)
                handoff_out[0, w, 0] = fresh.astype(BF16)
                return 0

            lax.fori_loop(0, terms, one, 0)

        totals = take_scalars(ITERS, energy_copies)
        energy_out[...] = jnp.broadcast_to(totals[1:2] / totals[0:1], (1, 128))

    square = (width, width)
    vmem = pl.BlockSpec(memory_space=pltpu.VMEM)
    smem = pl.BlockSpec(memory_space=pltpu.SMEM)
    anywhere = pl.BlockSpec(memory_space=pl.ANY)
    others = terms_axis - 1
    dma = pltpu.SemaphoreType.DMA
    return pl.pallas_call(
        kernel,
        out_shape=(
            jax.ShapeDtypeStruct((1, 1) + square, BF16),
            jax.ShapeDtypeStruct((1, 128), F32),
            jax.ShapeDtypeStruct((1, terms, 1) + square, BF16),
        ),
        in_specs=[vmem, anywhere, anywhere, smem, smem, smem, smem],
        out_specs=(vmem, vmem, vmem),
        scratch_shapes=[
            pltpu.VMEM((terms,) + square, BF16),
            pltpu.VMEM((terms,) + square, BF16),
            pltpu.VMEM((terms,) + square, BF16),
        ]
        + [pltpu.VMEM((sectors,) + square, BF16)] * gathers
        + [
            pltpu.VMEM(square, BF16),
            pltpu.VMEM(square, F32),
            pltpu.VMEM(square, BF16),
            pltpu.VMEM((ITERS, others, quarter, width), BF16),
            pltpu.VMEM((quarter, width), F32),
            pltpu.VMEM((quarter, width), F32),
            pltpu.VMEM((quarter, width), F32),
            pltpu.VMEM((gathers, sectors, 8, 128), F32),
            pltpu.VMEM((gathers, terms_axis, 8, 128), F32),
            pltpu.VMEM(square, BF16),
            pltpu.VMEM(square, BF16),
            dma((2,)),
            dma((2,)),
            dma((2, 2, ring - 1)),
            dma((2, 2, others, n_chunks)),
            dma((2, 2, terms_axis, n_chunks)),
            dma((2, 2, others)),
            dma((2, 2, sectors - 1)),
            dma((2, 2, others)),
            dma((2, others)),
            dma((2, terms_axis)),
        ],
        compiler_params=pltpu.CompilerParams(
            collective_id=1, has_side_effects=True, vmem_limit_bytes=48 * 1024 * 1024
        ),
    )


def solution(mesh):
    def local(two_site, left_env, right_env, block_dims, sources, sixj_index, sixj_table):
        call = build(
            mesh.shape["chain"], mesh.shape["sector"], mesh.shape["term"],
            left_env.shape[1], sources.shape[2], two_site.shape[2],
        )
        state, energy, handoff = call(
            two_site, left_env, right_env, block_dims, sources, sixj_index, sixj_table
        )
        return state, energy[0, 0:1], handoff

    return jax.shard_map(
        local,
        mesh=mesh,
        in_specs=(
            P("chain", "sector", None, None),
            P("chain", "term", "sector", None, None),
            P("chain", "term", "sector", None, None),
            P("sector"),
            P("term", "sector", None),
            P("term", "sector", None),
            P(),
        ),
        out_specs=(
            P("chain", "sector", None, None),
            P("chain"),
            P("chain", "term", "sector", None, None),
        ),
        check_vma=False,
    )
```

time: 814 us -> 160 us (0.20)
  waiting for transfers between devices: 447 us -> 0 us
  blocking collectives: 253 us -> 0 us
  Pallas kernels: 0 us -> 150 us
  matrix products: 41.2 us -> 0 us
  other arithmetic: 25.7 us -> 0 us
  between operations: 26.4 us -> 2.46 us
    psum x10 -> x0, blocking collectives: 253 us -> none  [totals(): return lax.psum(stacked, 'sector')]
    psum x5 -> x0, waiting for transfers between devices: 248 us -> none  [reduce_image(): lax.psum(partial_value.astype(jnp.bfloat16), 'term').astype(jnp.float32)]
    all_gather x5 -> x0, waiting for transfers between devices: 199 us -> none  [partial_image(): gathered = lax.all_gather(rounded_whole, 'sector', axis=0, tiled=True)]
    pallas_call x0 -> x1, Pallas kernels: none -> 150 us  [local(): call(two_site, left_env, right_env, block_dims, sources, sixj_index, sixj...]
    dot_general x11 -> x0, matrix products: 41.2 us -> none  [the longest x5 21 us: partial_image(): jnp.einsum('wba,aij->wbij', coupling, gathered, preferred_element_type=jn...]
    reduce_sum x12 -> x0, other arithmetic: 16.2 us -> none  [the longest x5 8.3 us: local(): summed = totals(jnp.stack([jnp.sum(state * image), jnp.sum(state * state)]))]
  transfers between devices with their start and end apart: 11 -> 0, of which waited for: 10 -> 0; matrix products, arithmetic and copies ran while one was open for 2% -> 0% of each run, Pallas kernels for 0% -> 0%
where the time goes in v1:
time: 160 us
  Pallas kernels  150 us (94%)
  local copies, waits for them, and re-layouts  7.49 us (5%)
  between operations  2.46 us (2%)
    pallas_call x1, Pallas kernels, local(): call(two_site, left_env, right_env, block_dims, sources, sixj_index, sixj...  150 us
    unnamed x12, local copies, waits for them, and re-layouts  7.49 us

profile of v1, /device:TPU:24, one launch (start us, length us, event | category | flops | bytes accessed | tf_op | source)
XLA Modules:
  0.0 159.6 jit_solution(12149409998168193387)
XLA Ops:
  1.3 0.8 copy.10.sources
  2.0 0.8 copy.11.sixj_index
  2.8 0.0 copy-start
  2.8 1.3 copy-done
  4.1 0.0 copy-start.1
  4.1 1.3 copy-done.1
  5.4 0.0 copy-start.2
  5.5 0.9 copy-done.2
  6.4 0.0 copy-start.3
  6.4 0.7 copy-done.3
  7.1 149.7 %shard_map.94 = (bf16[1,1,256,256]{3,2,1,0:T(8,128)(2,1)S(1)}, f32[1,128]{1,0:T(1,128)S(1)}, bf16[1,10,1,256,256]{4,3,2,1,0:T(8,128)(2,1)S(1)}) custom-call(f32[1,1,256,256]{3,2,1,0:T(8,128)S(1)} %copy-done.2, bf16[1,10,1,256,256]{4,3,2,1,0:T(8,128)(2,1)S(1)} %copy-done, bf16[1,10,1,256,256]{4,3,2,1,0:T(8,128)(2,1)S(1)} %copy-done.1, s32[1]{0:T(128)S(6)} %copy.15.dims, ...), custom_call_target="tpu_custom_call" | custom-call | tf_op jit(solution)/shard_map/pallas_call | solution.py:371
  156.8 0.7 copy.16
  157.5 1.1 copy.18
Async XLA Ops:
  2.8 1.3 copy-start
  4.1 1.3 copy-start.1
  5.4 0.9 copy-start.2
  6.4 0.7 copy-start.3

commit v2 on v1

v2 whole, which is shorter than its diff:
```python
import jax
import jax.numpy as jnp
from jax import lax
from jax.experimental import pallas as pl
from jax.experimental.pallas import tpu as pltpu
from jax.sharding import PartitionSpec as P

ITERS = 4
STEP = 0.1
EPSILON = 1e-06
MESH = pl.DeviceIdType.MESH
F32 = jnp.float32
BF16 = jnp.bfloat16


def place(distance, ring):
    half = ring // 2
    return jnp.where(
        distance == 0,
        0,
        jnp.where(
            distance < half,
            2 * distance - 1,
            jnp.where(distance == half, ring - 1, 2 * (ring - distance)),
        ),
    )


def place_static(distance, ring):
    half = ring // 2
    if distance == 0:
        return 0
    if distance < half:
        return 2 * distance - 1
    return ring - 1 if distance == half else 2 * (ring - distance)


def build(segments, sectors, terms_axis, terms, couplings, levels, width):
    ring = sectors // 2
    quarter = width // terms_axis
    gathers = ITERS + 1
    volume = float(sectors * width * width)
    chunks = [(0, 1)]
    for reach in range(1, ring // 2):
        chunks.append((2 * reach - 1, 2))
    chunks.append((ring - 1, 1))
    near_first = sorted(range(1, ring), key=lambda d: place_static(d, ring))
    late = 16
    turn_at = 3
    n_chunks = len(chunks)

    def kernel(
        two_site_hbm, left_hbm, right_hbm, dims_hbm, sources_hbm, index_hbm, table_hbm,
        solution_out, energy_out, handoff_out,
        two_site, dims, sources, sixj_index, sixj_table, left, right, previous, g0, g1, g2, g3, g4, mixed, right_part, part, outgoing, arrived,
        state_ref, image_ref, next_ref, scalars, scalars_term, block, previous_block,
        load_sem, left_sems, z_sems, x_sems, core_sems, rs_sems, sz_sems, sx_sems, sol_sems, sol_y_sems,
    ):
        gathered = (g0, g1, g2, g3, g4)
        y = lax.axis_index("chain")
        b = lax.axis_index("sector")
        t = lax.axis_index("term")
        z = b // 2
        c = b % 2

        def wrap(value, count):
            return lax.rem(value + count, count)

        def at_term(step):
            return (y, b, wrap(t + step, terms_axis))

        def at_sector(dz, dc):
            return (y, wrap(z + dz, ring) * 2 + wrap(c + dc, 2), t)

        def at_segment(dy, dt):
            return (wrap(y + dy, segments), b, wrap(t + dt, terms_axis))

        term_steps = (1, terms_axis - 1) + tuple(range(2, terms_axis - 1))
        sector_steps = [(dz, dc) for dz in range(ring) for dc in range(2) if (dz, dc) != (0, 0)]
        my_rows = pl.ds(pl.multiple_of(t * quarter, quarter), quarter)

        def rows_of(step):
            owner = wrap(t + step, terms_axis)
            return pl.ds(pl.multiple_of(owner * quarter, quarter), quarter)

        load_left = pltpu.make_async_copy(left_hbm.at[0, :, 0], left, load_sem.at[0])
        load_right = pltpu.make_async_copy(right_hbm.at[0, :, 0], right, load_sem.at[1])
        small = [
            pltpu.make_async_copy(source, target, load_sem.at[2 + i])
            for i, (source, target) in enumerate([
                (two_site_hbm.at[0, 0], two_site), (dims_hbm, dims), (sources_hbm, sources),
                (index_hbm, sixj_index), (table_hbm, sixj_table),
            ])
        ]
        for copy in small:
            copy.start()
        load_right.start()
        load_left.start()

        barrier = pltpu.get_barrier_semaphore()
        for step in term_steps:
            pl.semaphore_signal(barrier, inc=1, device_id=at_term(step), device_id_type=MESH)
        for dz, dc in sector_steps:
            pl.semaphore_signal(barrier, inc=1, device_id=at_sector(dz, dc), device_id_type=MESH)
        for dt in range(terms_axis):
            pl.semaphore_signal(barrier, inc=1, device_id=at_segment(-1, dt), device_id_type=MESH)

        def remote(source, target, sems, index, device):
            copy = pltpu.make_async_remote_copy(
                src_ref=source,
                dst_ref=target,
                send_sem=sems.at[(0,) + index],
                recv_sem=sems.at[(1,) + index],
                device_id=device,
                device_id_type=MESH,
            )
            copy.start()
            return copy

        for copy in small:
            copy.wait()
        limit = dims[0]
        row_ids = lax.broadcasted_iota(jnp.int32, (quarter, width), 0) + t * quarter
        column_ids = lax.broadcasted_iota(jnp.int32, (quarter, width), 1)
        mask = jnp.where((row_ids < limit) & (column_ids < limit), 1.0, 0.0).astype(F32)

        state = two_site[my_rows, :] * mask
        state_ref[...] = state
        gathered[0][0, t] = state.astype(BF16)

        pl.semaphore_wait(barrier, len(term_steps) + len(sector_steps) + terms_axis)

        lanes = lax.broadcasted_iota(jnp.int32, (1, 128), 1)

        def fold(value):
            return jnp.sum(jnp.sum(value, axis=0, keepdims=True), axis=1, keepdims=True)

        def send_scalars(k, values):
            packed = jnp.zeros((1, 128), F32)
            for i, value in enumerate(values):
                packed = jnp.where(lanes == i, value, packed)
            scalars[k, b] = packed
            return [
                remote(scalars.at[k, b], scalars.at[k, b], sz_sems, (k % 2, i), at_sector(dz, dc))
                for i, (dz, dc) in enumerate(sector_steps)
            ]

        def pass_scalars(k, copies):
            for copy in copies:
                copy.wait()
            scalars_term[k, t] = jnp.sum(scalars[k], axis=0)
            return [
                remote(scalars_term.at[k, t], scalars_term.at[k, t], sx_sems, (k % 2, i), at_term(step))
                for i, step in enumerate(term_steps)
            ]

        def take_scalars(k, copies, count):
            for copy in copies:
                copy.wait()
            total = jnp.sum(scalars_term[k], axis=0)
            return [
                jnp.sum(jnp.where(lanes == i, total, 0.0), axis=1, keepdims=True) for i in range(count)
            ]

        def gather(k, values, use_totals):
            whole = gathered[k]
            parity = k % 2
            x_copies, z_copies, late_copies, core_copies = {}, {}, {}, []
            everything = pl.ds(0, quarter)

            def early_rows(hops):
                return {1: 0, 2: quarter - late}.get(hops, quarter)

            def hops_of(distance):
                return min(distance, ring - distance)

            def members(index):
                first, count = chunks[index]
                return [
                    d for d in range(1, ring) if first <= place_static(ring - d, ring) < first + count
                ]

            def to_terms(index, rows):
                first, count = chunks[index]
                piece = whole.at[pl.ds(first, count), t, rows]
                for i, step in enumerate(term_steps):
                    x_copies[index, i] = remote(piece, piece, x_sems, (parity, i, index), at_term(step))

            def to_core(index):
                first, count = chunks[index]
                core_copies.append(
                    remote(
                        whole.at[pl.ds(first, count)], whole.at[pl.ds(ring + first, count)],
                        core_sems, (parity, index), at_sector(0, 1),
                    )
                )

            to_terms(0, everything)
            for distance in near_first:
                count = early_rows(hops_of(distance))
                if count:
                    z_copies[distance] = remote(
                        whole.at[0, t, pl.ds(0, count)],
                        whole.at[place_static(ring - distance, ring), t, pl.ds(0, count)],
                        z_sems, (parity, 0, distance - 1), at_sector(distance, 0),
                    )
            scalar_copies = send_scalars(k - 1, values) if k else None

            def turn():
                for i in range(len(term_steps)):
                    x_copies[0, i].wait_recv()
                for distance in near_first:
                    count = early_rows(hops_of(distance))
                    if count < quarter:
                        rows = pl.ds(count, quarter - count)
                        late_copies[distance] = remote(
                            whole.at[0, :, rows],
                            whole.at[place_static(ring - distance, ring), :, rows],
                            z_sems, (parity, 1, distance - 1), at_sector(distance, 0),
                        )
                to_core(0)

            for index in range(2, n_chunks):
                if index == turn_at:
                    turn()
                for distance in members(index):
                    z_copies[distance].wait_recv()
                to_terms(index, pl.ds(0, early_rows(hops_of(members(index)[0]))))
            if k:
                scalar_copies = pass_scalars(k - 1, scalar_copies)
            for index in range(1, n_chunks):
                for distance in members(index):
                    if distance in late_copies:
                        late_copies[distance].wait_recv()
                if index > 1:
                    for i in range(len(term_steps)):
                        x_copies[index, i].wait_recv()
                to_core(index)
                if k and index == n_chunks - 2:
                    use_totals(take_scalars(k - 1, scalar_copies, 3))
            for copy in core_copies:
                copy.wait_recv()
            sent = list(z_copies.values()) + list(late_copies.values()) + list(x_copies.values())
            return sent + core_copies

        def sector_place(sector):
            return wrap(sector % 2 + c, 2) * ring + place(wrap(sector // 2 - z + ring, ring), ring)

        def apply_terms(whole):
            for w in range(terms):
                spots = [sector_place(sources[i, 0, w]) for i in range(couplings)]
                weights = [sixj_table[sixj_index[i, 0, w]] for i in range(couplings)]
                for q in range(terms_axis):
                    total = weights[0] * whole[spots[0], q].astype(F32)
                    for i in range(1, couplings):
                        total = total + weights[i] * whole[spots[i], q].astype(F32)
                    mixed[w, pl.ds(q * quarter, quarter), :] = total.astype(BF16)
                right_part[w] = jnp.dot(mixed[w], right[w], preferred_element_type=F32).astype(BF16)
            total = None
            for w in range(terms):
                product = jnp.dot(left[w], right_part[w], preferred_element_type=F32)
                total = product if total is None else total + product
            part[...] = total

        def reduce_image(k):
            outgoing[...] = part[...].astype(BF16)
            copies = [
                remote(outgoing.at[rows_of(step)], arrived.at[k, i], rs_sems, (k % 2, i), at_term(step))
                for i, step in enumerate(term_steps)
            ]
            total = part[my_rows, :]
            for i, copy in enumerate(copies):
                copy.wait()
                total = total + arrived[k, i].astype(F32)
            return total * mask

        def corrected(k, totals, shift):
            norm, cross, square = totals
            delta = 1.0 - cross / norm
            grown = square + 2.0 * delta * cross + delta * delta * norm
            if k == 0:
                scale = lax.rsqrt(norm / volume + EPSILON)
                sigma = scale * lax.rsqrt(scale * scale * (grown / volume) + EPSILON)
            else:
                sigma = lax.rsqrt(grown / volume + EPSILON)
            state = sigma * (next_ref[...] + delta * state_ref[...])
            state_ref[...] = state
            return delta, sigma, shift + delta, state

        load_left.wait()
        left_copy = remote(left, previous, left_sems, (), at_segment(1, 0))
        load_right.wait()

        known = {"shift": jnp.zeros((1, 1), F32)}

        def step_totals(k):
            def use(totals):
                known["delta"], known["sigma"], known["shift"], _ = corrected(k, totals, known["shift"])

            return use

        values = None
        for k in range(ITERS):
            sent = gather(k, values, step_totals(k - 1))
            apply_terms(gathered[k])
            image = reduce_image(k)
            if k:
                image = known["sigma"] * (image + known["delta"] * image_ref[...])
            image_ref[...] = image
            state = state_ref[...]
            following = (1.0 + known["shift"]) * state - STEP * image
            next_ref[...] = following
            gathered[k + 1][0, t] = following.astype(BF16)
            values = [fold(state * state), fold(following * state), fold(following * following)]
            for copy in sent:
                copy.wait_send()

        block_copies, onward = [], []

        def last_totals(totals):
            known["delta"], known["sigma"], _, state = corrected(ITERS - 1, totals, known["shift"])
            block[my_rows, :] = state.astype(BF16)
            for i, step in enumerate(term_steps):
                block_copies.append(
                    remote(block.at[my_rows], block.at[my_rows], sol_sems, (i,), at_term(step))
                )
            for dt in range(terms_axis):
                onward.append(
                    remote(
                        block.at[my_rows], previous_block.at[my_rows],
                        sol_y_sems, (dt,), at_segment(1, dt),
                    )
                )

        sent = gather(ITERS, values, last_totals)
        apply_terms(gathered[ITERS])
        for copy in block_copies:
            copy.wait()
        solution_out[0, 0] = block[...]
        state = state_ref[...]
        overlap = fold(part[...] * block[...].astype(F32))
        overlap = known["sigma"] * (overlap + known["delta"] * fold(state * image_ref[...]))
        energy_copies = send_scalars(ITERS, [fold(state * state), overlap])
        for copy in sent:
            copy.wait_send()

        left_copy.wait()
        for copy in onward:
            copy.wait()

        @pl.when(y == 0)
        def _():
            handoff_out[0, :, 0] = left[...]

        @pl.when(y != 0)
        def _():
            turned = mixed.at[0]
            turned[...] = previous_block[...].T
            for w in range(terms):
                inner = jnp.dot(previous[w], previous_block[...], preferred_element_type=F32)
                right_part[w] = inner.astype(BF16)
            for w in range(terms):
                fresh = jnp.dot(turned[...], right_part[w], preferred_element_type=F32)
                handoff_out[0, w, 0] = (fresh * (1.0 / width**0.5)).astype(BF16)

        energy_copies = pass_scalars(ITERS, energy_copies)
        norm, overlap = take_scalars(ITERS, energy_copies, 2)
        energy_out[...] = jnp.broadcast_to(overlap / norm, (1, 128))

    square = (width, width)
    vmem = pl.BlockSpec(memory_space=pltpu.VMEM)
    smem = pltpu.SMEM
    held = pl.BlockSpec(memory_space=pl.ANY)
    others = terms_axis - 1
    dma = pltpu.SemaphoreType.DMA
    return pl.pallas_call(
        kernel,
        out_shape=(
            jax.ShapeDtypeStruct((1, 1) + square, BF16),
            jax.ShapeDtypeStruct((1, 128), F32),
            jax.ShapeDtypeStruct((1, terms, 1) + square, BF16),
        ),
        in_specs=[held] * 7,
        out_specs=(vmem, vmem, vmem),
        scratch_shapes=[
            pltpu.VMEM(square, F32),
            smem((1,), jnp.int32),
            smem((couplings, 1, terms), jnp.int32),
            smem((couplings, 1, terms), jnp.int32),
            smem((levels,), F32),
            pltpu.VMEM((terms,) + square, BF16),
            pltpu.VMEM((terms,) + square, BF16),
            pltpu.VMEM((terms,) + square, BF16),
        ]
        + [pltpu.VMEM((sectors, terms_axis, quarter, width), BF16)] * gathers
        + [
            pltpu.VMEM((terms,) + square, BF16),
            pltpu.VMEM((terms,) + square, BF16),
            pltpu.VMEM(square, F32),
            pltpu.VMEM(square, BF16),
            pltpu.VMEM((ITERS, others, quarter, width), BF16),
            pltpu.VMEM((quarter, width), F32),
            pltpu.VMEM((quarter, width), F32),
            pltpu.VMEM((quarter, width), F32),
            pltpu.VMEM((gathers, sectors, 1, 128), F32),
            pltpu.VMEM((gathers, terms_axis, 1, 128), F32),
            pltpu.VMEM(square, BF16),
            pltpu.VMEM(square, BF16),
            dma((7,)),
            dma((2,)),
            dma((2, 2, 2, ring - 1)),
            dma((2, 2, others, n_chunks)),
            dma((2, 2, n_chunks)),
            dma((2, 2, others)),
            dma((2, 2, sectors - 1)),
            dma((2, 2, others)),
            dma((2, others)),
            dma((2, terms_axis)),
        ],
        compiler_params=pltpu.CompilerParams(
            collective_id=1, has_side_effects=True, vmem_limit_bytes=56500 * 1024
        ),
    )


def hand_over(state, energy, handoff):
    terms = handoff.shape[1]

    def kernel(state_in, energy_in, handoff_in, state_out, energy_out, handoff_out, a, b, c, sems):
        moves = [(state_in, a, state_out), (energy_in, b, energy_out)] + [
            (handoff_in.at[0, w], c.at[0, w], handoff_out.at[0, w]) for w in range(terms)
        ]
        loads = [pltpu.make_async_copy(m[0], m[1], sems.at[0, i]) for i, m in enumerate(moves)]
        stores = [pltpu.make_async_copy(m[1], m[2], sems.at[1, i]) for i, m in enumerate(moves)]
        for copy in loads:
            copy.start()
        for load, store in zip(loads, stores):
            load.wait()
            store.start()
        for copy in stores:
            copy.wait()

    held = pl.BlockSpec(memory_space=pl.ANY)
    arrays = (state, energy, handoff)
    return pl.pallas_call(
        kernel,
        out_shape=tuple(jax.ShapeDtypeStruct(array.shape, array.dtype) for array in arrays),
        in_specs=[held] * 3,
        out_specs=(held,) * 3,
        scratch_shapes=[pltpu.VMEM(array.shape, array.dtype) for array in arrays]
        + [pltpu.SemaphoreType.DMA((2, terms + 2))],
        compiler_params=pltpu.CompilerParams(vmem_limit_bytes=56500 * 1024),
    )(*arrays)


def solution(mesh):
    def local(two_site, left_env, right_env, block_dims, sources, sixj_index, sixj_table):
        call = build(
            mesh.shape["chain"], mesh.shape["sector"], mesh.shape["term"],
            left_env.shape[1], sources.shape[2], sixj_table.shape[0], two_site.shape[2],
        )
        state, energy, handoff = call(
            two_site, left_env, right_env, block_dims, sources.transpose(2, 1, 0),
            sixj_index.transpose(2, 1, 0), sixj_table
        )
        state, energy, handoff = hand_over(state, energy, handoff)
        return state, energy[0, 0:1], handoff

    return jax.shard_map(
        local,
        mesh=mesh,
        in_specs=(
            P("chain", "sector", None, None),
            P("chain", "term", "sector", None, None),
            P("chain", "term", "sector", None, None),
            P("sector"),
            P("term", "sector", None),
            P("term", "sector", None),
            P(),
        ),
        out_specs=(
            P("chain", "sector", None, None),
            P("chain"),
            P("chain", "term", "sector", None, None),
        ),
        check_vma=False,
    )
```

time: 160 us -> 129 us (0.81)
  the two profiles are of different devices: /device:TPU:24 before, /device:TPU:40 now
where the time goes in v2:
time: 129 us; the launch traced here: 128 us
  Pallas kernels  127 us (98%)
  between operations  1.29 us (1%)
    pallas_call x1, Pallas kernels, local(): call(two_site, left_env, right_env, block_dims, sources.transpose(2, 1, 0...  125 us

profile of v2, /device:TPU:40, one launch (start us, length us, event | category | flops | bytes accessed | tf_op | source)
XLA Modules:
  0.0 128.4 jit_solution(7251203235043494018)
XLA Ops:
  1.3 124.8 %shard_map.94 = (bf16[1,1,256,256]{3,2,1,0:T(8,128)(2,1)}, f32[1,128]{1,0:T(1,128)}, bf16[1,10,1,256,256]{4,3,2,1,0:T(8,128)(2,1)}) custom-call(f32[1,1,256,256]{3,2,1,0:T(8,128)} %two_site_hbm.1, bf16[1,10,1,256,256]{4,3,2,1,0:T(8,128)(2,1)} %left_hbm.1, bf16[1,10,1,256,256]{4,3,2,1,0:T(8,128)(2,1)} %right_hbm.1, s32[1]{0:T(128)S(6)} %copy.10.dims_hbm, ...), custom_call_target="tpu_custom_call" | custom-call | tf_op jit(solution)/shard_map/pallas_call | solution.py:462
  126.1 2.3 %shard_map.95 = (bf16[1,1,256,256]{3,2,1,0:T(8,128)(2,1)}, f32[1,128]{1,0:T(1,128)}, bf16[1,10,1,256,256]{4,3,2,1,0:T(8,128)(2,1)}) custom-call(bf16[1,1,256,256]{3,2,1,0:T(8,128)(2,1)} %get-tuple-element.9.state_in, f32[1,128]{1,0:T(1,128)} %get-tuple-element.10.energy_in, bf16[1,10,1,256,256]{4,3,2,1,0:T(8,128)(2,1)} %get-tuple-element.11.handoff_in), custom_call_target="tpu_custom_call" | custom-call | tf_op jit(solution)/shard_map/pallas_call | solution.py:445

commit v3 on v2

v3 whole, which is shorter than its diff:
```python
import jax
import jax.numpy as jnp
from jax import lax
from jax.experimental import pallas as pl
from jax.experimental.pallas import tpu as pltpu
from jax.sharding import PartitionSpec as P

ITERS = 4
STEP = 0.1
EPSILON = 1e-06
MESH = pl.DeviceIdType.MESH
F32 = jnp.float32
BF16 = jnp.bfloat16


def place(distance, ring):
    half = ring // 2
    return jnp.where(
        distance == 0,
        0,
        jnp.where(
            distance < half,
            2 * distance - 1,
            jnp.where(distance == half, ring - 1, 2 * (ring - distance)),
        ),
    )


def place_static(distance, ring):
    half = ring // 2
    if distance == 0:
        return 0
    if distance < half:
        return 2 * distance - 1
    return ring - 1 if distance == half else 2 * (ring - distance)


def build(segments, sectors, terms_axis, terms, couplings, levels, width):
    ring = sectors // 2
    half = width // 2
    strip = half // terms_axis
    quarter = 2 * strip
    gathers = ITERS + 1
    volume = float(sectors * width * width)
    chunks = [(0, 1)]
    for reach in range(1, ring // 2):
        chunks.append((2 * reach - 1, 2))
    chunks.append((ring - 1, 1))
    near_first = sorted(range(1, ring), key=lambda d: place_static(d, ring))
    late = 16
    turn_at = 2
    n_chunks = len(chunks)

    def kernel(
        two_site_hbm, left_hbm, right_hbm, dims_hbm, sources_hbm, index_hbm, table_hbm,
        solution_out, energy_out, handoff_out,
        two_site, dims, sources, sixj_index, sixj_table, left_whole, left, right, previous, g0, g1, g2, g3, g4,
        other_half, mixed, right_part, part, outgoing, arrived, turned,
        state_ref, image_ref, next_ref, scalars, scalars_term, block, previous_block,
        load_sem, left_sems, pair_sems, z_sems, late_sems, own_sems, x_sems, rs_sems, sz_sems, sx_sems, sol_sems, sol_y_sems,
    ):
        gathered = (g0, g1, g2, g3, g4)
        y = lax.axis_index("chain")
        b = lax.axis_index("sector")
        t = lax.axis_index("term")
        z = b // 2
        c = b % 2

        def wrap(value, count):
            return lax.rem(value + count, count)

        def at_term(step):
            return (y, b, wrap(t + step, terms_axis))

        def at_sector(dz, dc):
            return (y, wrap(z + dz, ring) * 2 + wrap(c + dc, 2), t)

        def at_segment(dy, dt):
            return (wrap(y + dy, segments), b, wrap(t + dt, terms_axis))

        term_steps = (1, terms_axis - 1) + tuple(range(2, terms_axis - 1))
        sector_steps = [(dz, dc) for dz in range(ring) for dc in range(2) if (dz, dc) != (0, 0)]
        chip_steps = [
            (dt, dc) for dc in range(2) for dt in (0,) + term_steps if (dt, dc) != (0, 0)
        ]

        def at_chip(dt, dc):
            return (y, z * 2 + wrap(c + dc, 2), wrap(t + dt, terms_axis))

        def my_strips(ref):
            low = ref[pl.ds(pl.multiple_of(t * strip, strip), strip), :]
            high = ref[pl.ds(pl.multiple_of(half + t * strip, strip), strip), :]
            return jnp.concatenate([low, high], axis=0)

        def left_half(core):
            return left_hbm.at[0, :, 0, :, pl.ds(pl.multiple_of(core * half, half), half)]

        load_whole = pltpu.make_async_copy(left_hbm.at[0, :, 0], left_whole, load_sem.at[7])
        load_left = pltpu.make_async_copy(left_half(c), left.at[c], load_sem.at[0])
        load_right = pltpu.make_async_copy(right_hbm.at[0, :, 0], right.at[c], load_sem.at[1])
        small = [
            pltpu.make_async_copy(source, target, load_sem.at[2 + i])
            for i, (source, target) in enumerate([
                (two_site_hbm.at[0, 0], two_site), (dims_hbm, dims), (sources_hbm, sources.at[c]),
                (index_hbm, sixj_index.at[c]), (table_hbm, sixj_table),
            ])
        ]
        for copy in small:
            copy.start()
        load_right.start()
        load_whole.start()
        load_left.start()

        barrier = pltpu.get_barrier_semaphore()
        for step in term_steps:
            for dc in range(2):
                pl.semaphore_signal(barrier, inc=1, device_id=at_chip(step, dc), device_id_type=MESH)
        for dz, dc in sector_steps:
            pl.semaphore_signal(barrier, inc=1, device_id=at_sector(dz, dc), device_id_type=MESH)
        for dt in range(terms_axis):
            pl.semaphore_signal(barrier, inc=1, device_id=at_segment(-1, dt), device_id_type=MESH)

        def remote(source, target, sems, index, device):
            copy = pltpu.make_async_remote_copy(
                src_ref=source,
                dst_ref=target,
                send_sem=sems.at[(0,) + index],
                recv_sem=sems.at[(1,) + index],
                device_id=device,
                device_id_type=MESH,
            )
            copy.start()
            return copy

        for copy in small:
            copy.wait()
        limit = dims[0]
        row_ids = lax.broadcasted_iota(jnp.int32, (quarter, width), 0)
        row_ids = t * strip + jnp.where(row_ids < strip, row_ids, row_ids - strip + half)
        column_ids = lax.broadcasted_iota(jnp.int32, (quarter, width), 1)
        mask = jnp.where((row_ids < limit) & (column_ids < limit), 1.0, 0.0).astype(F32)

        def stage(k, value):
            low, high = value[0:strip], value[strip:quarter]
            gathered[k][c, t] = jnp.where(c == 0, low, high).astype(BF16)
            other_half[k] = jnp.where(c == 0, high, low).astype(BF16)

        state = my_strips(two_site) * mask
        state_ref[...] = state
        stage(0, state)

        pl.semaphore_wait(barrier, 2 * len(term_steps) + len(sector_steps) + terms_axis)

        lanes = lax.broadcasted_iota(jnp.int32, (1, 128), 1)

        def fold(value):
            return jnp.sum(jnp.sum(value, axis=0, keepdims=True), axis=1, keepdims=True)

        def send_scalars(k, values):
            packed = jnp.zeros((1, 128), F32)
            for i, value in enumerate(values):
                packed = jnp.where(lanes == i, value, packed)
            scalars[k, b] = packed
            return [
                remote(scalars.at[k, b], scalars.at[k, b], sz_sems, (k % 2, i), at_sector(dz, dc))
                for i, (dz, dc) in enumerate(sector_steps)
            ]

        def pass_scalars(k, copies):
            for copy in copies:
                copy.wait()
            scalars_term[k, t] = jnp.sum(scalars[k], axis=0)
            return [
                remote(scalars_term.at[k, t], scalars_term.at[k, t], sx_sems, (k % 2, i), at_term(step))
                for i, step in enumerate(term_steps)
            ]

        def take_scalars(k, copies, count):
            for copy in copies:
                copy.wait()
            total = jnp.sum(scalars_term[k], axis=0)
            return [
                jnp.sum(jnp.where(lanes == i, total, 0.0), axis=1, keepdims=True) for i in range(count)
            ]

        def gather(k, values, use_totals, before):
            whole = gathered[k]
            other = other_half.at[k]
            parity = k % 2
            x_copies, z_copies, late_copies = {}, {}, {}

            def early_rows(hops):
                return {1: 0, 2: strip - late}.get(hops, strip)

            def hops_of(distance):
                return min(distance, ring - distance)

            def members(index):
                first, count = chunks[index]
                return [
                    d for d in range(1, ring) if first <= place_static(ring - d, ring) < first + count
                ]

            own_copies = [remote(other, whole.at[c, t], own_sems, (parity, 0, 0), at_sector(0, 1))]
            for i, step in enumerate(term_steps):
                own_copies.append(
                    remote(
                        whole.at[c, t], whole.at[c, t], own_sems, (parity, 0, 1 + i), at_chip(step, 0)
                    )
                )
                own_copies.append(
                    remote(other, whole.at[c, t], own_sems, (parity, 1, 1 + i), at_chip(step, 1))
                )
            for distance in near_first:
                count = early_rows(hops_of(distance))
                if count:
                    rows = pl.ds(0, count)
                    target = whole.at[2 * place_static(ring - distance, ring) + c, t, rows]
                    z_copies[distance] = [
                        remote(
                            whole.at[c, t, rows], target,
                            z_sems, (parity, 0, distance - 1), at_sector(distance, 0),
                        ),
                        remote(
                            other.at[rows], target,
                            z_sems, (parity, 1, distance - 1), at_sector(distance, 1),
                        ),
                    ]
            scalar_copies = send_scalars(k - 1, values()) if k else send_environments()

            def turn():
                for copy in own_copies:
                    copy.wait_recv()
                for distance in near_first:
                    count = early_rows(hops_of(distance))
                    if count < strip:
                        rows = pl.ds(count, strip - count)
                        late_copies[distance] = remote(
                            whole.at[pl.ds(0, 2), :, rows],
                            whole.at[pl.ds(2 * place_static(ring - distance, ring), 2), :, rows],
                            late_sems, (parity, distance - 1), at_sector(distance, 0),
                        )

            for index in range(2, n_chunks):
                if index == turn_at:
                    turn()
                for distance in members(index):
                    for copy in z_copies[distance]:
                        copy.wait_recv()
                first, count = chunks[index]
                rows = pl.ds(0, early_rows(hops_of(members(index)[0])))
                piece = whole.at[pl.ds(2 * first, 2 * count), t, rows]
                for i, step in enumerate(term_steps):
                    x_copies[index, i] = remote(piece, piece, x_sems, (parity, i, index), at_term(step))
            if k:
                scalar_copies = pass_scalars(k - 1, scalar_copies)
            for copy in before:
                copy.wait_send()
            for index in range(1, n_chunks):
                if k and index == n_chunks - 1:
                    use_totals(take_scalars(k - 1, scalar_copies, 3))
                for distance in members(index):
                    if distance in late_copies:
                        late_copies[distance].wait_recv()
                if index > 1:
                    for i in range(len(term_steps)):
                        x_copies[index, i].wait_recv()
            sent = own_copies + list(late_copies.values()) + list(x_copies.values())
            return sent + [copy for pair in z_copies.values() for copy in pair]

        def sector_place(sector):
            return 2 * place(wrap(sector // 2 - z + ring, ring), ring) + sector % 2

        def apply_terms(whole, send=None):
            for turn_of in range(2):
                s = wrap(c + 1 - turn_of, 2)
                for w in range(terms):
                    spots = [sector_place(sources[s, i, 0, w]) for i in range(couplings)]
                    weights = [sixj_table[sixj_index[s, i, 0, w]] for i in range(couplings)]
                    for q in range(terms_axis):
                        total = weights[0] * whole[spots[0], q].astype(F32)
                        for i in range(1, couplings):
                            total = total + weights[i] * whole[spots[i], q].astype(F32)
                        mixed[turn_of, w, pl.ds(q * strip, strip), :] = total.astype(BF16)
                    product = jnp.dot(mixed[turn_of, w], right[s, w], preferred_element_type=F32)
                    right_part[turn_of, w // 2, pl.ds(w % 2 * half, half), :] = product.astype(BF16)
                total = None
                for p in range(terms // 2):
                    both = jnp.concatenate([left[s, 2 * p], left[s, 2 * p + 1]], axis=1)
                    product = jnp.dot(both, right_part[turn_of, p], preferred_element_type=F32)
                    total = product if total is None else total + product
                part[turn_of] = total
                if send is not None:
                    send(turn_of)

        def image_of(k, whole):
            copies = []

            def send(turn_of):
                outgoing[turn_of] = part[turn_of].astype(BF16).reshape(2, terms_axis, strip, width)
                for i, (dt, dc) in enumerate(chip_steps):
                    if dc == 1 - turn_of:
                        copies.append(
                            remote(
                                outgoing.at[turn_of, :, wrap(t + dt, terms_axis)], arrived.at[k, i],
                                rs_sems, (k % 2, i), at_chip(dt, dc),
                            )
                        )

            apply_terms(whole, send)
            total = my_strips(part.at[1])
            for copy in copies:
                copy.wait()
            for i in range(len(chip_steps)):
                total = total + arrived[k, i].astype(F32).reshape(quarter, width)
            return total * mask

        def corrected(k, totals, shift):
            norm, cross, square = totals
            delta = 1.0 - cross / norm
            grown = square + 2.0 * delta * cross + delta * delta * norm
            if k == 0:
                scale = lax.rsqrt(norm / volume + EPSILON)
                sigma = scale * lax.rsqrt(scale * scale * (grown / volume) + EPSILON)
            else:
                sigma = lax.rsqrt(grown / volume + EPSILON)
            state = sigma * (next_ref[...] + delta * state_ref[...])
            state_ref[...] = state
            return delta, sigma, shift + delta, state

        sibling = at_sector(0, 1)
        other_columns = pl.ds(pl.multiple_of((1 - c) * half, half), half)
        pair_copies = [
            remote(sources_hbm, sources.at[c], pair_sems, (0,), sibling),
            remote(index_hbm, sixj_index.at[c], pair_sems, (1,), sibling),
        ]

        def send_environments():
            load_right.wait()
            pair_copies.append(remote(right.at[c], right.at[c], pair_sems, (2,), sibling))
            load_whole.wait()
            pair_copies.append(
                remote(left_whole.at[:, :, other_columns], left.at[c], pair_sems, (3,), sibling)
            )
            pair_copies.append(remote(left_whole, previous, left_sems, (), at_segment(1, 0)))
            load_left.wait()

        known = {"shift": jnp.zeros((1, 1), F32)}

        def step_totals(k):
            def use(totals):
                known["delta"], known["sigma"], known["shift"], _ = corrected(k, totals, known["shift"])

            return use

        values, sent = None, []
        for k in range(ITERS):
            sent = gather(k, values, step_totals(k - 1), sent)
            if k == 0:
                for copy in pair_copies[0:4]:
                    copy.wait()
            image = image_of(k, gathered[k])
            if k:
                image = known["sigma"] * (image + known["delta"] * image_ref[...])
            image_ref[...] = image
            state = state_ref[...]
            following = (1.0 + known["shift"]) * state - STEP * image
            next_ref[...] = following
            stage(k + 1, following)

            def values(state=state, following=following):
                return [fold(state * state), fold(following * state), fold(following * following)]


        block_copies, onward = [], []

        def last_totals(totals):
            known["delta"], known["sigma"], _, state = corrected(ITERS - 1, totals, known["shift"])
            block[c, :, t] = state.astype(BF16).reshape(2, strip, width)
            mine = block.at[c, :, t]
            for i, (dt, dc) in enumerate(chip_steps):
                block_copies.append(remote(mine, mine, sol_sems, (i,), at_chip(dt, dc)))
            for dt in range(terms_axis):
                onward.append(
                    remote(mine, previous_block.at[:, t], sol_y_sems, (dt,), at_segment(1, dt))
                )

        sent = gather(ITERS, values, last_totals, sent)
        apply_terms(gathered[ITERS])
        for copy in block_copies:
            copy.wait()
        solution_out[0, 0] = block[c].reshape(width, width)
        state = state_ref[...]
        overlap = part[0] * block[1 - c].reshape(width, width).astype(F32)
        overlap = fold(overlap + part[1] * block[c].reshape(width, width).astype(F32))
        overlap = known["sigma"] * (overlap + known["delta"] * fold(state * image_ref[...]))
        energy_copies = send_scalars(ITERS, [fold(state * state), overlap])
        for copy in sent:
            copy.wait_send()

        pair_copies[4].wait()
        for copy in onward:
            copy.wait()

        @pl.when(y == 0)
        def _():
            handoff_out[0, :, 0] = left_whole[...]

        @pl.when(y != 0)
        def _():
            received = previous_block[...].reshape(width, width)
            turned[...] = received.T
            for w in range(terms):
                inner = jnp.dot(previous[w], received, preferred_element_type=F32)
                right_part[w % 2, w // 2] = inner.astype(BF16)
            for w in range(terms):
                fresh = jnp.dot(turned[...], right_part[w % 2, w // 2], preferred_element_type=F32)
                handoff_out[0, w, 0] = (fresh * (1.0 / width**0.5)).astype(BF16)

        energy_copies = pass_scalars(ITERS, energy_copies)
        norm, overlap = take_scalars(ITERS, energy_copies, 2)
        energy_out[...] = jnp.broadcast_to(overlap / norm, (1, 128))

    square = (width, width)
    vmem = pl.BlockSpec(memory_space=pltpu.VMEM)
    smem = pltpu.SMEM
    held = pl.BlockSpec(memory_space=pl.ANY)
    others = terms_axis - 1
    peers = 2 * terms_axis - 1
    dma = pltpu.SemaphoreType.DMA
    return pl.pallas_call(
        kernel,
        out_shape=(
            jax.ShapeDtypeStruct((1, 1) + square, BF16),
            jax.ShapeDtypeStruct((1, 128), F32),
            jax.ShapeDtypeStruct((1, terms, 1) + square, BF16),
        ),
        in_specs=[held] * 7,
        out_specs=(vmem, vmem, vmem),
        scratch_shapes=[
            pltpu.VMEM(square, F32),
            smem((1,), jnp.int32),
            smem((2, couplings, 1, terms), jnp.int32),
            smem((2, couplings, 1, terms), jnp.int32),
            smem((levels,), F32),
            pltpu.VMEM((terms,) + square, BF16),
            pltpu.VMEM((2, terms, width, half), BF16),
            pltpu.VMEM((2, terms) + square, BF16),
            pltpu.VMEM((terms,) + square, BF16),
        ]
        + [pltpu.VMEM((sectors, terms_axis, strip, width), BF16)] * gathers
        + [
            pltpu.VMEM((gathers, strip, width), BF16),
            pltpu.VMEM((2, terms, half, width), BF16),
            pltpu.VMEM((2, terms // 2) + square, BF16),
            pltpu.VMEM((2,) + square, F32),
            pltpu.VMEM((2, 2, terms_axis, strip, width), BF16),
            pltpu.VMEM((ITERS, peers, 2, strip, width), BF16),
            pltpu.VMEM(square, BF16),
            pltpu.VMEM((quarter, width), F32),
            pltpu.VMEM((quarter, width), F32),
            pltpu.VMEM((quarter, width), F32),
            pltpu.VMEM((gathers, sectors, 1, 128), F32),
            pltpu.VMEM((gathers, terms_axis, 1, 128), F32),
            pltpu.VMEM((2, 2, terms_axis, strip, width), BF16),
            pltpu.VMEM((2, terms_axis, strip, width), BF16),
            dma((8,)),
            dma((2,)),
            dma((2, 4)),
            dma((2, 2, 2, ring - 1)),
            dma((2, 2, ring - 1)),
            dma((2, 2, 2, terms_axis)),
            dma((2, 2, others, n_chunks)),
            dma((2, 2, peers)),
            dma((2, 2, sectors - 1)),
            dma((2, 2, others)),
            dma((2, peers)),
            dma((2, terms_axis)),
        ],
        compiler_params=pltpu.CompilerParams(
            collective_id=1, has_side_effects=True, vmem_limit_bytes=56500 * 1024
        ),
    )


def hand_over(state, energy, handoff):
    terms = handoff.shape[1]

    def kernel(state_in, energy_in, handoff_in, state_out, energy_out, handoff_out, a, b, c, sems):
        moves = [(state_in, a, state_out), (energy_in, b, energy_out)] + [
            (handoff_in.at[0, w], c.at[0, w], handoff_out.at[0, w]) for w in range(terms)
        ]
        loads = [pltpu.make_async_copy(m[0], m[1], sems.at[0, i]) for i, m in enumerate(moves)]
        stores = [pltpu.make_async_copy(m[1], m[2], sems.at[1, i]) for i, m in enumerate(moves)]
        for copy in loads:
            copy.start()
        for load, store in zip(loads, stores):
            load.wait()
            store.start()
        for copy in stores:
            copy.wait()

    held = pl.BlockSpec(memory_space=pl.ANY)
    arrays = (state, energy, handoff)
    return pl.pallas_call(
        kernel,
        out_shape=tuple(jax.ShapeDtypeStruct(array.shape, array.dtype) for array in arrays),
        in_specs=[held] * 3,
        out_specs=(held,) * 3,
        scratch_shapes=[pltpu.VMEM(array.shape, array.dtype) for array in arrays]
        + [pltpu.SemaphoreType.DMA((2, terms + 2))],
        compiler_params=pltpu.CompilerParams(vmem_limit_bytes=56500 * 1024),
    )(*arrays)


def solution(mesh):
    def local(two_site, left_env, right_env, block_dims, sources, sixj_index, sixj_table):
        call = build(
            mesh.shape["chain"], mesh.shape["sector"], mesh.shape["term"],
            left_env.shape[1], sources.shape[2], sixj_table.shape[0], two_site.shape[2],
        )
        state, energy, handoff = call(
            two_site, left_env, right_env, block_dims, sources.transpose(2, 1, 0),
            sixj_index.transpose(2, 1, 0), sixj_table
        )
        state, energy, handoff = hand_over(state, energy, handoff)
        return state, energy[0, 0:1], handoff

    return jax.shard_map(
        local,
        mesh=mesh,
        in_specs=(
            P("chain", "sector", None, None),
            P("chain", "term", "sector", None, None),
            P("chain", "term", "sector", None, None),
            P("sector"),
            P("term", "sector", None),
            P("term", "sector", None),
            P(),
        ),
        out_specs=(
            P("chain", "sector", None, None),
            P("chain"),
            P("chain", "term", "sector", None, None),
        ),
        check_vma=False,
    )
```

time: 129 us -> 126 us (0.977)
  the two profiles are of different devices: /device:TPU:40 before, /device:TPU:24 now
where the time goes in v3:
time: 126 us
  Pallas kernels  125 us (99%)
  between operations  1.29 us (1%)
    pallas_call x1, Pallas kernels, local(): call(two_site, left_env, right_env, block_dims, sources.transpose(2, 1, 0...  123 us

profile of v3, /device:TPU:24, one launch (start us, length us, event | category | flops | bytes accessed | tf_op | source)
XLA Modules:
  0.0 126.2 jit_solution(6383475578265574649)
XLA Ops:
  1.3 122.6 %shard_map.94 = (bf16[1,1,256,256]{3,2,1,0:T(8,128)(2,1)}, f32[1,128]{1,0:T(1,128)}, bf16[1,10,1,256,256]{4,3,2,1,0:T(8,128)(2,1)}) custom-call(f32[1,1,256,256]{3,2,1,0:T(8,128)} %two_site_hbm.1, bf16[1,10,1,256,256]{4,3,2,1,0:T(8,128)(2,1)} %left_hbm.1, bf16[1,10,1,256,256]{4,3,2,1,0:T(8,128)(2,1)} %right_hbm.1, s32[1]{0:T(128)S(6)} %copy.10.dims_hbm, ...), custom_call_target="tpu_custom_call" | custom-call | tf_op jit(solution)/shard_map/pallas_call | solution.py:522
  123.9 2.3 %shard_map.95 = (bf16[1,1,256,256]{3,2,1,0:T(8,128)(2,1)}, f32[1,128]{1,0:T(1,128)}, bf16[1,10,1,256,256]{4,3,2,1,0:T(8,128)(2,1)}) custom-call(bf16[1,1,256,256]{3,2,1,0:T(8,128)(2,1)} %get-tuple-element.9.state_in, f32[1,128]{1,0:T(1,128)} %get-tuple-element.10.energy_in, bf16[1,10,1,256,256]{4,3,2,1,0:T(8,128)(2,1)} %get-tuple-element.11.handoff_in), custom_call_target="tpu_custom_call" | custom-call | tf_op jit(solution)/shard_map/pallas_call | solution.py:505

commit v4 on v3

--- a/solution.py
+++ b/solution.py
@@ -55,7 +55,7 @@
         two_site_hbm, left_hbm, right_hbm, dims_hbm, sources_hbm, index_hbm, table_hbm,
         solution_out, energy_out, handoff_out,
         two_site, dims, sources, sixj_index, sixj_table, left_whole, left, right, previous, g0, g1, g2, g3, g4,
-        other_half, mixed, right_part, part, outgoing, arrived, turned,
+        other_half, mixed, right_part, part, outgoing, arrived, turned, solved,
         state_ref, image_ref, next_ref, scalars, scalars_term, block, previous_block,
         load_sem, left_sems, pair_sems, z_sems, late_sems, own_sems, x_sems, rs_sems, sz_sems, sx_sems, sol_sems, sol_y_sems,
     ):
@@ -389,7 +389,9 @@
         apply_terms(gathered[ITERS])
         for copy in block_copies:
             copy.wait()
-        solution_out[0, 0] = block[c].reshape(width, width)
+        solved[...] = block[c].reshape(width, width)
+        solved_copy = pltpu.make_async_copy(solved, solution_out.at[0, 0], load_sem.at[0])
+        solved_copy.start()
         state = state_ref[...]
         overlap = part[0] * block[1 - c].reshape(width, width).astype(F32)
         overlap = fold(overlap + part[1] * block[c].reshape(width, width).astype(F32))
@@ -404,7 +406,9 @@
 
         @pl.when(y == 0)
         def _():
-            handoff_out[0, :, 0] = left_whole[...]
+            copy = pltpu.make_async_copy(left_whole, handoff_out.at[0, :, 0], load_sem.at[1])
+            copy.start()
+            copy.wait()
 
         @pl.when(y != 0)
         def _():
@@ -415,10 +419,14 @@
                 right_part[w % 2, w // 2] = inner.astype(BF16)
             for w in range(terms):
                 fresh = jnp.dot(turned[...], right_part[w % 2, w // 2], preferred_element_type=F32)
-                handoff_out[0, w, 0] = (fresh * (1.0 / width**0.5)).astype(BF16)
+                previous[w] = (fresh * (1.0 / width**0.5)).astype(BF16)
+            copy = pltpu.make_async_copy(previous, handoff_out.at[0, :, 0], load_sem.at[1])
+            copy.start()
+            copy.wait()
 
         energy_copies = pass_scalars(ITERS, energy_copies)
         norm, overlap = take_scalars(ITERS, energy_copies, 2)
+        solved_copy.wait()
         energy_out[...] = jnp.broadcast_to(overlap / norm, (1, 128))
 
     square = (width, width)
@@ -436,7 +444,7 @@
             jax.ShapeDtypeStruct((1, terms, 1) + square, BF16),
         ),
         in_specs=[held] * 7,
-        out_specs=(vmem, vmem, vmem),
+        out_specs=(held, vmem, held),
         scratch_shapes=[
             pltpu.VMEM(square, F32),
             smem((1,), jnp.int32),
@@ -456,6 +464,7 @@
             pltpu.VMEM((2,) + square, F32),
             pltpu.VMEM((2, 2, terms_axis, strip, width), BF16),
             pltpu.VMEM((ITERS, peers, 2, strip, width), BF16),
+            pltpu.VMEM(square, BF16),
             pltpu.VMEM(square, BF16),
             pltpu.VMEM((quarter, width), F32),
             pltpu.VMEM((quarter, width), F32),

time: 126 us -> 126 us (level)
  no operation moved by 1% of the time
where the time goes in v4:
time: 126 us
  Pallas kernels  124 us (98%)
  between operations  1.29 us (1%)
    pallas_call x1, Pallas kernels, local(): call(two_site, left_env, right_env, block_dims, sources.transpose(2, 1, 0...  122 us

profile of v4, /device:TPU:24, one launch (start us, length us, event | category | flops | bytes accessed | tf_op | source)
XLA Modules:
  0.0 125.8 jit_solution(7836104225243223827)
XLA Ops:
  1.3 122.2 %shard_map.94 = (bf16[1,1,256,256]{3,2,1,0:T(8,128)(2,1)}, f32[1,128]{1,0:T(1,128)}, bf16[1,10,1,256,256]{4,3,2,1,0:T(8,128)(2,1)}) custom-call(f32[1,1,256,256]{3,2,1,0:T(8,128)} %two_site_hbm.1, bf16[1,10,1,256,256]{4,3,2,1,0:T(8,128)(2,1)} %left_hbm.1, bf16[1,10,1,256,256]{4,3,2,1,0:T(8,128)(2,1)} %right_hbm.1, s32[1]{0:T(128)S(6)} %copy.10.dims_hbm, ...), custom_call_target="tpu_custom_call" | custom-call | tf_op jit(solution)/shard_map/pallas_call | solution.py:531
  123.5 2.3 %shard_map.95 = (bf16[1,1,256,256]{3,2,1,0:T(8,128)(2,1)}, f32[1,128]{1,0:T(1,128)}, bf16[1,10,1,256,256]{4,3,2,1,0:T(8,128)(2,1)}) custom-call(bf16[1,1,256,256]{3,2,1,0:T(8,128)(2,1)} %get-tuple-element.9.state_in, f32[1,128]{1,0:T(1,128)} %get-tuple-element.10.energy_in, bf16[1,10,1,256,256]{4,3,2,1,0:T(8,128)(2,1)} %get-tuple-element.11.handoff_in), custom_call_target="tpu_custom_call" | custom-call | tf_op jit(solution)/shard_map/pallas_call | solution.py:514

commit v5 on v4

--- a/solution.py
+++ b/solution.py
@@ -257,7 +257,7 @@
             for copy in before:
                 copy.wait_send()
             for index in range(1, n_chunks):
-                if k and index == n_chunks - 1:
+                if k == ITERS and index == n_chunks - 1:
                     use_totals(take_scalars(k - 1, scalar_copies, 3))
                 for distance in members(index):
                     if distance in late_copies:
@@ -265,6 +265,8 @@
                 if index > 1:
                     for i in range(len(term_steps)):
                         x_copies[index, i].wait_recv()
+            if 0 < k < ITERS:
+                use_totals(take_scalars(k - 1, scalar_copies, 3))
             sent = own_copies + list(late_copies.values()) + list(x_copies.values())
             return sent + [copy for pair in z_copies.values() for copy in pair]
 

time: 126 us -> 126 us (level)
  no operation moved by 1% of the time
where the time goes in v5:
time: 126 us; the launch traced here: 125 us
  Pallas kernels  124 us (98%)
  between operations  1.29 us (1%)
    pallas_call x1, Pallas kernels, local(): call(two_site, left_env, right_env, block_dims, sources.transpose(2, 1, 0...  122 us

profile of v5, /device:TPU:24, one launch (start us, length us, event | category | flops | bytes accessed | tf_op | source)
XLA Modules:
  0.0 125.4 jit_solution(11205230612659947238)
XLA Ops:
  1.3 121.8 %shard_map.94 = (bf16[1,1,256,256]{3,2,1,0:T(8,128)(2,1)}, f32[1,128]{1,0:T(1,128)}, bf16[1,10,1,256,256]{4,3,2,1,0:T(8,128)(2,1)}) custom-call(f32[1,1,256,256]{3,2,1,0:T(8,128)} %two_site_hbm.1, bf16[1,10,1,256,256]{4,3,2,1,0:T(8,128)(2,1)} %left_hbm.1, bf16[1,10,1,256,256]{4,3,2,1,0:T(8,128)(2,1)} %right_hbm.1, s32[1]{0:T(128)S(6)} %copy.10.dims_hbm, ...), custom_call_target="tpu_custom_call" | custom-call | tf_op jit(solution)/shard_map/pallas_call | solution.py:533
  123.1 2.3 %shard_map.95 = (bf16[1,1,256,256]{3,2,1,0:T(8,128)(2,1)}, f32[1,128]{1,0:T(1,128)}, bf16[1,10,1,256,256]{4,3,2,1,0:T(8,128)(2,1)}) custom-call(bf16[1,1,256,256]{3,2,1,0:T(8,128)(2,1)} %get-tuple-element.9.state_in, f32[1,128]{1,0:T(1,128)} %get-tuple-element.10.energy_in, bf16[1,10,1,256,256]{4,3,2,1,0:T(8,128)(2,1)} %get-tuple-element.11.handoff_in), custom_call_target="tpu_custom_call" | custom-call | tf_op jit(solution)/shard_map/pallas_call | solution.py:516
